TPU v7x, 32 devices: a whole 2x2x4 slice. The times are simulated.
32 devices in a mesh: groups: 2 (over x), blk: 16 (over z, y, core).
Axes of the slice: x: 2, y: 2, z: 4, core: 2. Of those that a mesh axis runs over, the one named last changes fastest.
Arguments:
- queries: bfloat16 [32768, 1024], P(('groups', 'blk')), parts along dimension 0, may hold values from -2.5 to 2.5
- passages: bfloat16 [128, 256, 1024], P('blk', 'groups'), parts along dimension 1, may hold values from -12 to 12
- block_list: int32 [256, 4], P(('groups', 'blk')), parts along dimension 0, may hold values from 0 to 127, as said below
- pair_count: int32 [256], P(('groups', 'blk')), parts along dimension 0, may hold values from 1 to 4, 256 in all
- positive: int32 [32768], P(('groups', 'blk')), parts along dimension 0, may hold values from 0 to 511
Outputs:
- row_loss: float32 [32768], P(('groups', 'blk')), parts along dimension 0
- query_grad: bfloat16 [32768, 1024], P(('groups', 'blk')), parts along dimension 0
- passage_grad: bfloat16 [128, 256, 1024], P('blk', 'groups'), parts along dimension 1
There are 2 independent parts, one for each index of `groups`. A program takes and returns all parts, laid end to end along the dimension named above; each array names one. Nothing has to cross between parts.
Inputs may be any that keep to these rules, and one draw needn't show every extreme that they name: `block_list`: each row names 4 different passage blocks; the 8 rows of one index of blk (aligned runs of 8 rows) name exactly 8 different passage blocks in all, each of them in the same number of rows. `pair_count`: the 128 entries of one group sum to 256, and some entry of each group equals 4; the sum holds for each group separately, not over all groups together.
All inputs are finite; a program needn't handle non-finite values.
Results may differ from a plain program's by a relative error of at most 0.0039.
Values may be sent and summed in bfloat16 or wider, within the bound.
A program may use at most 128 MiB of HBM per device.

v0:
```python
import jax
import jax.numpy as jnp
from jax import lax
from jax.sharding import PartitionSpec as P

D = 1024
BLK = 128
NB = 4
DISTINCT = 8


def send_back(partial_value):
    return lax.all_to_all(partial_value, "blk", split_axis=0, concat_axis=1, tiled=True)


def body(queries, passages, block_list, pair_count, positive):
    qblocks_here = block_list.shape[0]
    listed = block_list.reshape(-1)
    pair_total = listed.shape[0]
    span_cols = NB * BLK
    ordered = jnp.sort(listed)
    fresh = jnp.concatenate([jnp.ones((1,), jnp.bool_), ordered[1:] != ordered[:-1]])
    rank_of = jnp.cumsum(fresh.astype(jnp.int32)) - 1
    wanted = jnp.full((DISTINCT,), -1, jnp.int32).at[rank_of].set(ordered)
    matches = listed[:, None] == wanted[None, :]
    slot_index = jnp.sum(
        matches.astype(jnp.int32) * jnp.arange(DISTINCT, dtype=jnp.int32)[None, :], axis=1
    )
    merge_table = matches.astype(jnp.float32)
    requests = lax.all_gather(jnp.maximum(wanted, 0), "blk", axis=0, tiled=True)
    served = passages[:, requests, :]
    fetched = lax.all_to_all(served, "blk", split_axis=1, concat_axis=0, tiled=True)
    candidates = fetched[:, slot_index, :].reshape(BLK, qblocks_here, NB, D)
    query_rows = queries.reshape(qblocks_here, BLK, D)
    scores = jnp.einsum(
        "grd,cgnd->grnc", query_rows, candidates, preferred_element_type=jnp.float32
    )
    scores = scores.reshape(qblocks_here, BLK, span_cols)
    columns = jnp.arange(span_cols, dtype=jnp.int32)
    live_limit = pair_count * BLK
    is_live = columns[None, None, :] < live_limit[:, None, None]
    target_slot = positive.reshape(qblocks_here, BLK) % live_limit[:, None]
    row_max = jnp.max(jnp.where(is_live, scores, -jnp.inf), axis=2, keepdims=True)
    weights = jnp.where(is_live, jnp.exp(scores - row_max), jnp.float32(0.0))
    row_sum = jnp.sum(weights, axis=2, keepdims=True)
    target = jnp.take_along_axis(scores, target_slot[:, :, None], axis=2)[:, :, 0]
    row_loss = row_max[:, :, 0] + jnp.log(row_sum[:, :, 0]) - target
    onehot = (columns[None, None, :] == target_slot[:, :, None]).astype(jnp.float32)
    grad_scores = (
        (weights / row_sum - onehot).astype(jnp.bfloat16).reshape(qblocks_here, BLK, NB, BLK)
    )
    contrib = jnp.einsum(
        "grnc,grd->cgnd", grad_scores, query_rows, preferred_element_type=jnp.float32
    )
    contrib = contrib.reshape(BLK, pair_total, D)
    partial_value = jnp.einsum("cpd,pk->ckd", contrib, merge_table, precision=lax.Precision.HIGHEST)
    query_grad = jnp.einsum(
        "grnc,cgnd->grd", grad_scores, candidates, preferred_element_type=jnp.float32
    ).astype(jnp.bfloat16)
    returned = send_back(partial_value)
    passage_grad = jnp.zeros(passages.shape, jnp.float32).at[:, requests, :].add(returned)
    return (row_loss.reshape(-1), query_grad.reshape(-1, D), passage_grad.astype(jnp.bfloat16))


def solution(mesh):
    return jax.shard_map(
        body,
        mesh=mesh,
        in_specs=(
            P(("groups", "blk"), None),
            P("blk", "groups", None),
            P(("groups", "blk"), None),
            P(("groups", "blk")),
            P(("groups", "blk")),
        ),
        out_specs=(P(("groups", "blk")), P(("groups", "blk"), None), P("blk", "groups", None)),
        check_vma=False,
    )
```

profile of v0, /device:TPU:15, one launch (start us, length us, event | category | flops | bytes accessed | tf_op | source)
XLA Modules:
  0.0 248.9 jit_solution(7454822869387522437)
XLA Ops:
  0.6 0.0 copy-start
  0.7 0.9 copy.39
  1.6 0.1 reshape.340
  1.6 1.6 sort.15
  3.2 0.1 compare_bitcast_fusion.2
  3.3 0.1 add_convert_fusion
  3.4 0.1 copy.40
  3.5 0.1 reduce-window.4
  3.6 0.1 fusion.9
  3.7 1.2 dynamic-slice
  5.6 0.7 scatter_custom_fusion
  6.3 0.1 maximum_dynamic-update-slice_fusion
  6.4 7.9 %all-reduce = s32[128]{0:T(128)S(1)} all-reduce(s32[128]{0:T(128)S(1)} %maximum_dynamic-update-slice_fusion), channel_id=1, replica_groups=mesh['groups'=2,'blk'=16] {'blk'}, use_global_device_ids=true, to_apply=%add | all-reduce | flops 128 | bytes 1024
  14.3 7.5 %gather_fusion = bf16[128,8,1024]{2,0,1:T(8,128)(2,1)} fusion(bf16[8,128,1024]{2,1,0:T(8,128)(2,1)} %param.6, s32[1024]{0:T(1024)S(1)} %pad_clamp_fusion.1), kind=kCustom, calls=%fused_computation | custom fusion | bytes 4194816 | tf_op jit(solution)/shard_map/gather | solution.py:31
  21.8 4.1 %copy.41 = bf16[8,128,1024]{2,0,1:T(8,128)(2,1)} copy(bf16[8,128,1024]{2,1,0:T(8,128)(2,1)} %bitcast.88) | data formatting | bytes 4194304 | tf_op jit(solution)/shard_map/gather | solution.py:31
  25.8 0.0 copy-start.3
  25.8 0.0 copy-start.2
  25.8 9.4 %all-to-all-start = ((bf16[8,128,1024]{2,0,1:T(8,128)(2,1)}), bf16[8,128,1024]{2,0,1:T(8,128)(2,1)}, u32[]{:S(2)}, u32[]{:S(2)}) async-start(bf16[8,128,1024]{2,0,1:T(8,128)(2,1)} %copy.41), calls=%async_computation | async-start | bytes 4194304 | tf_op jit(solution)/shard_map/all_to_all | solution.py:32
  35.3 0.1 fusion.11
  35.3 0.1 copy.44
  35.4 0.1 fusion.10
  35.6 0.0 copy-done.3
  35.6 0.1 broadcast_compare_fusion
  35.7 0.0 copy-done.2
  35.7 0.2 add_select_fusion
  35.9 46.9 %all-to-all-done = bf16[8,128,1024]{2,0,1:T(8,128)(2,1)} async-done(((bf16[8,128,1024]{2,0,1:T(8,128)(2,1)}), bf16[8,128,1024]{2,0,1:T(8,128)(2,1)}, u32[]{:S(2)}, u32[]{:S(2)}) %all-to-all-start) | async-done | bytes 2097184 | tf_op jit(solution)/shard_map/all_to_all | solution.py:32
  82.8 3.0 %copy.43 = bf16[16,8,8,1024]{3,2,1,0:T(8,128)(2,1)S(1)} copy(bf16[16,8,8,1024]{3,1,2,0:T(8,128)(2,1)} %bitcast.5) | data formatting | bytes 4194304 | tf_op jit(solution)/shard_map/all_to_all | solution.py:32
  85.8 2.5 copy.47
  88.3 6.5 %gather_fusion.1 = bf16[32,128,1024]{2,1,0:T(8,128)(2,1)} fusion(bf16[128,8,1024]{2,0,1:T(8,128)(2,1)} %copy.47, s32[1024]{0:T(1024)S(1)} %pad_clamp_fusion), kind=kCustom, calls=%fused_computation.1 | custom fusion | bytes 16777344 | tf_op jit(solution)/shard_map/gather | solution.py:33
  94.8 0.0 copy-done
  94.8 4.8 %fusion.5 = (f32[8,128]{1,0:T(8,128)S(1)}, f32[8,128,4,128]{3,1,2,0:T(8,128)S(1)}) fusion(pred[8,4,128]{2,1,0:T(4,128)(4,1)S(1)} %broadcast_compare_fusion, bf16[128,8,4,1024]{3,0,2,1:T(8,128)(2,1)} %bitcast.85, bf16[8,128,1024,1]{2,1,3,0:T(8,128)(2,1)S(1)} %bitcast.80), kind=kOutput, calls=%fused_computation.11 | convolution fusion | flops 1074789376 | bytes 12591104 | tf_op jit(solution)/shard_map/grd,cgnd->grnc/dot_general | solution.py:35
  99.6 0.0 copy-start.1
  99.6 0.7 fusion.8
  100.3 2.5 fusion.23
  102.8 0.0 copy-done.1
  102.8 13.3 %fusion.2 = f32[128,8,1024]{2,1,0:T(8,128)} fusion(f32[128,32,1024]{2,0,1:T(8,128)S(1)} %bitcast.82, s32[32]{0:T(128)S(1)} %reshape.340, s32[8]{0:T(128)S(1)} %scatter_custom_fusion), kind=kOutput, calls=%fused_computation.8 | convolution fusion | flops 402653440 | bytes 20971680 | tf_op jit(solution)/shard_map/cpd,pk->ckd/dot_general | solution.py:56
  116.1 4.9 %all-to-all-start.1 = ((f32[128,8,1024]{2,1,0:T(8,128)}), f32[128,8,1024]{2,1,0:T(8,128)}, u32[]{:S(2)}, u32[]{:S(2)}) async-start(f32[128,8,1024]{2,1,0:T(8,128)} %fusion.2), calls=%async_computation.1 | async-start | bytes 8388608 | tf_op jit(solution)/shard_map/all_to_all | solution.py:13
  121.0 0.2 compare_select_fusion.2
  121.3 14.8 %gather_fusion.2 = f32[1024]{0:T(1024)S(1)} fusion(f32[8,128,512]{1,2,0:T(8,128)} %bitcast.83, s32[1024]{0:T(1024)S(1)} %fusion.14), kind=kCustom, calls=%fused_computation.2 | custom fusion | bytes 20480 | tf_op jit(solution)/shard_map/jit(take_along_axis)/gather | solution.py:46
  136.0 0.1 rem.46
  136.1 0.7 bitcast_subtract_fusion.1
  136.8 7.3 %bitcast_convert_fusion = bf16[8,128,1024]{2,1,0:T(8,128)(2,1)} fusion(bf16[128,8,4,1024]{3,0,2,1:T(8,128)(2,1)} %bitcast.86, f32[8,128,4,128]{3,1,2,0:T(8,128)} %copy-done.1, s32[8,128]{1,0:T(8,128)S(1)} %add_select_fusion, s32[4,128]{1,0:T(4,128)S(1)} %multiply_add_fusion, f32[8,128]{1,0:T(8,128)S(1)} %fusion.8, f32[8,128]{1,0:T(8,128)S(1)} %get-tuple-element.20, ...), kind=kOutput, calls=%fused_computation.7 | convolution fusion | flops 1078460416 | bytes 12601344 | tf_op jit(solution)/shard_map/grnc,cgnd->grd/dot_general | solution.py:57
  144.2 69.3 %all-to-all-done.1 = f32[128,8,1024]{2,1,0:T(8,128)} async-done(((f32[128,8,1024]{2,1,0:T(8,128)}), f32[128,8,1024]{2,1,0:T(8,128)}, u32[]{:S(2)}, u32[]{:S(2)}) %all-to-all-start.1) | async-done | bytes 4194336 | tf_op jit(solution)/shard_map/all_to_all | solution.py:13
  213.5 7.7 %copy.50 = f32[8,16,8,1024]{3,0,2,1:T(8,128)} copy(f32[8,16,8,1024]{3,2,0,1:T(8,128)} %bitcast.33) | data formatting | bytes 8388608 | tf_op jit(solution)/shard_map/all_to_all | solution.py:13
  221.2 2.5 %broadcast_in_dim.50 = f32[8,128,1024]{2,0,1:T(8,128)} broadcast(f32[]{:T(128)} %constant.47.clone.1), dimensions={} | broadcast | bytes 4194308 | tf_op jit(solution)/shard_map/broadcast_in_dim | solution.py:61
  223.7 20.2 %scatter_fusion = f32[8,128,1024]{2,0,1:T(8,128)} fusion(f32[8,128,1024]{2,0,1:T(8,128)} %broadcast_in_dim.50, s32[128]{0:T(128)S(1)} %compare_select_fusion.6, f32[128,8,1024]{2,1,0:T(8,128)} %bitcast.84), kind=kCustom, calls=%fused_computation.4 | custom fusion | flops 1048576 | bytes 12583424 | tf_op jit(solution)/shard_map/scatter-add | solution.py:61
  243.9 2.5 %convert_element_type.30 = bf16[8,128,1024]{2,0,1:T(8,128)(2,1)S(1)} convert(f32[8,128,1024]{2,0,1:T(8,128)} %scatter_fusion) | non-fusion elementwise | flops 1048576 | bytes 6291456 | tf_op jit(solution)/shard_map/convert_element_type | solution.py:62
  246.4 2.5 copy.51
  (12 shorter events, 0.1 us)
Async XLA Ops:
  0.6 94.2 %copy-start = (bf16[1024,1024]{1,0:T(8,128)(2,1)S(1)}, bf16[1024,1024]{1,0:T(8,128)(2,1)}, u32[]{:S(2)}) copy-start(bf16[1024,1024]{1,0:T(8,128)(2,1)} %param.5) | copy-start | bytes 6291460
  25.8 9.7 %copy-start.3 = (s32[8]{0:T(128)S(1)}, s32[8]{0:T(128)}, u32[]{:S(2)}) copy-start(s32[8]{0:T(128)} %param.8) | copy-start | bytes 100
  25.8 9.8 %copy-start.2 = (s32[1024]{0:T(1024)S(1)}, s32[1024]{0:T(1024)}, u32[]{:S(2)}) copy-start(s32[1024]{0:T(1024)} %param.9) | copy-start | bytes 12292
  25.8 57.0 %all-to-all-start = ((bf16[8,128,1024]{2,0,1:T(8,128)(2,1)}), bf16[8,128,1024]{2,0,1:T(8,128)(2,1)}, u32[]{:S(2)}, u32[]{:S(2)}) async-start(bf16[8,128,1024]{2,0,1:T(8,128)(2,1)} %copy.41), calls=%async_computation | async-start | bytes 4194304 | tf_op jit(solution)/shard_map/all_to_all | solution.py:32
  99.6 3.2 %copy-start.1 = (f32[8,128,4,128]{3,1,2,0:T(8,128)}, f32[8,128,4,128]{3,1,2,0:T(8,128)S(1)}, u32[]{:S(2)}) copy-start(f32[8,128,4,128]{3,1,2,0:T(8,128)S(1)} %get-tuple-element.21) | copy-start | bytes 6291460
  116.1 97.4 %all-to-all-start.1 = ((f32[128,8,1024]{2,1,0:T(8,128)}), f32[128,8,1024]{2,1,0:T(8,128)}, u32[]{:S(2)}, u32[]{:S(2)}) async-start(f32[128,8,1024]{2,1,0:T(8,128)} %fusion.2), calls=%async_computation.1 | async-start | bytes 8388608 | tf_op jit(solution)/shard_map/all_to_all | solution.py:13
where the time goes:
time: 250 us; the launch traced here: 249 us
  waiting for transfers between devices  116 us (46%)
  local copies, waits for them, and re-layouts  54.2 us (22%)
  matrix products  27.9 us (11%)
  other arithmetic  26.9 us (11%)
  starting transfers between devices  14.3 us (6%)
  blocking collectives  7.89 us (3%)
    all_to_all x1, waiting for transfers between devices, send_back(): lax.all_to_all(partial_value, 'blk', split_axis=0, concat_axis=1, tiled=T...  69.3 us
    all_to_all x1, waiting for transfers between devices, body(): lax.all_to_all(served, 'blk', split_axis=1, concat_axis=0, tiled=True)  46.9 us
    scatter-add x1, other arithmetic, body(): jnp.zeros(passages.shape, jnp.float32).at[:, requests, :].add(returned)  20.2 us
    gather x1, local copies, waits for them, and re-layouts, body(): jnp.take_along_axis(scores, target_slot[:, :, None], axis=2)[:, :, 0]  14.8 us
    dot_general x1, matrix products, body(): jnp.einsum('cpd,pk->ckd', contrib, merge_table, precision=lax.Precision.H...  13.3 us
    gather x2, local copies, waits for them, and re-layouts, body(): served = passages[:, requests, :]  11.6 us
    all_to_all x1, starting transfers between devices, body(): lax.all_to_all(served, 'blk', split_axis=1, concat_axis=0, tiled=True)  9.42 us
    unnamed x1, blocking collectives  7.89 us
  transfers between devices with their start and end apart: 2, of which 2 were waited for; matrix products, arithmetic and copies ran while one was open for 10% of the time, Pallas kernels for 0%

commit v1 on v0

--- a/solution.py
+++ b/solution.py
@@ -29,7 +29,15 @@
     merge_table = matches.astype(jnp.float32)
     requests = lax.all_gather(jnp.maximum(wanted, 0), "blk", axis=0, tiled=True)
     served = passages[:, requests, :]
-    fetched = lax.all_to_all(served, "blk", split_axis=1, concat_axis=0, tiled=True)
+    ways, here = (lax.axis_size("blk"), lax.axis_index("blk"))
+    width = served.shape[1] // ways
+    turned = jnp.roll(served, -here * width, axis=1)
+    got = [lax.slice_in_dim(turned, 0, width, axis=1)]
+    for far in range(1, ways):
+        sent = lax.slice_in_dim(turned, far * width, (far + 1) * width, axis=1)
+        got.append(lax.ppermute(sent, "blk", [(d, (d + far) % ways) for d in range(ways)]))
+    line = jnp.concatenate(got[::-1], axis=0)
+    fetched = jnp.roll(line, (here + 1) * got[0].shape[0], axis=0)
     candidates = fetched[:, slot_index, :].reshape(BLK, qblocks_here, NB, D)
     query_rows = queries.reshape(qblocks_here, BLK, D)
     scores = jnp.einsum(

time: 250 us -> 265 us (1.060)
  starting transfers between devices: 14.3 us -> 42.8 us
  waiting for transfers between devices: 116 us -> 95.1 us
  other arithmetic: 26.9 us -> 34.6 us
    all_to_all x1 -> x0, waiting for transfers between devices: 46.9 us -> none  [body(): lax.all_to_all(served, 'blk', split_axis=1, concat_axis=0, tiled=True)]
    ppermute x0 -> x15, starting transfers between devices: none -> 32.2 us  [body(): lax.ppermute(sent, 'blk', [(d, (d + far) % ways) for d in range(ways)])]
    ppermute x0 -> x15, waiting for transfers between devices: none -> 25.9 us  [body(): lax.ppermute(sent, 'blk', [(d, (d + far) % ways) for d in range(ways)])]
    all_to_all x1 -> x0, starting transfers between devices: 9.42 us -> none  [body(): lax.all_to_all(served, 'blk', split_axis=1, concat_axis=0, tiled=True)]
    all_to_all x1, starting transfers between devices: 4.91 us -> 10.6 us  [send_back(): lax.all_to_all(partial_value, 'blk', split_axis=0, concat_axis=1, tiled=T...]
    all_to_all x2 -> x0, local copies, waits for them, and re-layouts: 5.47 us -> none  [body(): lax.all_to_all(served, 'blk', split_axis=1, concat_axis=0, tiled=True)]
    gather x2 -> x1, local copies, waits for them, and re-layouts: 11.6 us -> 7.54 us  [body(): served = passages[:, requests, :]]
    unnamed x14 -> x65, local copies, waits for them, and re-layouts: 4.65 us -> 7.81 us
  transfers between devices with their start and end apart: 2 -> 16, of which waited for: 2 -> 10; matrix products, arithmetic and copies ran while one was open for 10% -> 11% of each run, Pallas kernels for 0% -> 0%
where the time goes in v1:
time: 265 us; the launch traced here: 264 us
  waiting for transfers between devices  95.1 us (36%)
  local copies, waits for them, and re-layouts  54.1 us (20%)
  starting transfers between devices  42.8 us (16%)
  other arithmetic  34.6 us (13%)
  matrix products  27.7 us (10%)
  blocking collectives  7.88 us (3%)
    all_to_all x1, waiting for transfers between devices, send_back(): lax.all_to_all(partial_value, 'blk', split_axis=0, concat_axis=1, tiled=T...  69.2 us
    ppermute x15, starting transfers between devices, body(): lax.ppermute(sent, 'blk', [(d, (d + far) % ways) for d in range(ways)])  32.2 us
    ppermute x15, waiting for transfers between devices, body(): lax.ppermute(sent, 'blk', [(d, (d + far) % ways) for d in range(ways)])  25.9 us
    scatter-add x1, other arithmetic, body(): jnp.zeros(passages.shape, jnp.float32).at[:, requests, :].add(returned)  20.4 us
    gather x1, local copies, waits for them, and re-layouts, body(): jnp.take_along_axis(scores, target_slot[:, :, None], axis=2)[:, :, 0]  14.8 us
    dot_general x1, matrix products, body(): jnp.einsum('cpd,pk->ckd', contrib, merge_table, precision=lax.Precision.H...  13.1 us
    all_to_all x1, starting transfers between devices, send_back(): lax.all_to_all(partial_value, 'blk', split_axis=0, concat_axis=1, tiled=T...  10.6 us
    unnamed x1, blocking collectives  7.88 us
  transfers between devices with their start and end apart: 16, of which 10 were waited for; matrix products, arithmetic and copies ran while one was open for 11% of the time, Pallas kernels for 0%

profile of v1, /device:TPU:15, one launch (start us, length us, event | category | flops | bytes accessed | tf_op | source)
XLA Modules:
  0.0 263.9 jit_solution(10511193232225717617)
XLA Ops:
  0.7 0.9 copy.19
  1.6 0.1 reshape.340
  1.7 1.6 sort.15
  3.3 0.1 compare_bitcast_fusion.2
  3.3 0.1 add_convert_fusion
  3.4 0.1 copy.20
  3.6 0.1 fusion.10
  3.7 1.2 dynamic-slice
  5.6 0.7 scatter_custom_fusion
  6.3 1.2 broadcast_multiply_fusion
  7.5 7.9 %all-reduce = s32[128]{0:T(128)S(1)} all-reduce(s32[128]{0:T(128)S(1)} %get-tuple-element.31), channel_id=1, replica_groups=mesh['groups'=2,'blk'=16] {'blk'}, use_global_device_ids=true, to_apply=%add | all-reduce | flops 128 | bytes 1024
  15.4 0.6 copy-done.7
  16.0 7.5 %gather_fusion = bf16[128,8,1024]{2,0,1:T(8,128)(2,1)} fusion(bf16[8,128,1024]{2,1,0:T(8,128)(2,1)} %param.6, s32[1024]{0:T(1024)S(1)} %pad_clamp_fusion.1), kind=kCustom, calls=%fused_computation | custom fusion | bytes 4194816 | tf_op jit(solution)/shard_map/gather | solution.py:31
  23.5 2.7 %fusion.5 = bf16[8,128,1024]{2,1,0:T(8,128)(2,1)S(1)} fusion(s32[]{:T(128)S(6)} %select_n.134, bf16[8,128,1024]{2,1,0:T(8,128)(2,1)} %bitcast.83), kind=kLoop, calls=%fused_computation.11 | loop fusion | flops 4194304 | bytes 4194308 | tf_op jit(solution)/shard_map/jit(_roll_dynamic)/concatenate | solution.py:34
  26.3 1.3 copy-done.3
  27.6 1.0 fusion.25
  28.6 4.0 %collective-permute-start.14 = (bf16[8,8,1024]{2,1,0:T(8,128)(2,1)S(1)}, bf16[8,8,1024]{2,1,0:T(8,128)(2,1)S(1)}, u32[]{:S(2)}, u32[]{:S(2)}) collective-permute-start(bf16[8,8,1024]{2,1,0:T(8,128)(2,1)S(1)} %get-tuple-element.12), channel_id=1, source_target_pairs={{0,1},{1,2},{2,3},{3,4},{4,5},{5,6},{6,7},{7,8},{8,9},{9,10},{10,1... | collective-permute-start | bytes 393224 | tf_op jit(solution)/shard_map/ppermute | solution.py:38
  32.6 0.6 collective-permute-start.13
  33.1 0.9 collective-permute-start.1
  34.0 1.3 collective-permute-start
  35.3 0.5 broadcast_compare_fusion.1
  35.8 0.6 fusion.12
  36.4 1.3 copy.21
  37.8 0.7 broadcast_compare_fusion
  38.5 0.8 add_select_fusion
  39.3 0.8 fusion.11
  40.1 0.6 pad_clamp_fusion
  40.7 1.7 collective-permute-done
  42.5 3.1 %collective-permute-start.3 = (bf16[8,8,1024]{2,1,0:T(8,128)(2,1)}, bf16[8,8,1024]{2,1,0:T(8,128)(2,1)S(1)}, u32[]{:S(2)}, u32[]{:S(2)}) collective-permute-start(bf16[8,8,1024]{2,1,0:T(8,128)(2,1)} %get-tuple-element.23), channel_id=1, source_target_pairs={{0,12},{1,13},{2,14},{3,15},{4,0},{5,1},{6,2},{7,3},{8,4},{9,5},{1... | collective-permute-start | bytes 393224 | tf_op jit(solution)/shard_map/ppermute | solution.py:38
  45.6 3.2 %collective-permute-done.2 = bf16[8,8,1024]{2,1,0:T(8,128)(2,1)S(1)} collective-permute-done((bf16[8,8,1024]{2,1,0:T(8,128)(2,1)}, bf16[8,8,1024]{2,1,0:T(8,128)(2,1)S(1)}, u32[]{:S(2)}, u32[]{:S(2)}) %collective-permute-start.2) | collective-permute-done | bytes 131104 | tf_op jit(solution)/shard_map/ppermute | solution.py:38
  48.8 3.4 %collective-permute-start.4 = (bf16[8,8,1024]{2,1,0:T(8,128)(2,1)}, bf16[8,8,1024]{2,1,0:T(8,128)(2,1)S(1)}, u32[]{:S(2)}, u32[]{:S(2)}) collective-permute-start(bf16[8,8,1024]{2,1,0:T(8,128)(2,1)} %get-tuple-element.22), channel_id=1, source_target_pairs={{0,11},{1,12},{2,13},{3,14},{4,15},{5,0},{6,1},{7,2},{8,3},{9,4},{... | collective-permute-start | bytes 393224 | tf_op jit(solution)/shard_map/ppermute | solution.py:38
  52.3 2.5 collective-permute-start.5
  54.8 0.9 collective-permute-done.4
  55.7 1.7 collective-permute-start.6
  57.4 2.1 collective-permute-done.5
  59.5 8.4 %collective-permute-start.7 = (bf16[8,8,1024]{2,1,0:T(8,128)(2,1)}, bf16[8,8,1024]{2,1,0:T(8,128)(2,1)S(1)}, u32[]{:S(2)}, u32[]{:S(2)}) collective-permute-start(bf16[8,8,1024]{2,1,0:T(8,128)(2,1)} %get-tuple-element.19), channel_id=1, source_target_pairs={{0,8},{1,9},{2,10},{3,11},{4,12},{5,13},{6,14},{7,15},{8,0},{9,1},... | collective-permute-start | bytes 393224 | tf_op jit(solution)/shard_map/ppermute | solution.py:38
  68.0 3.1 %collective-permute-start.8 = (bf16[8,8,1024]{2,1,0:T(8,128)(2,1)}, bf16[8,8,1024]{2,1,0:T(8,128)(2,1)S(1)}, u32[]{:S(2)}, u32[]{:S(2)}) collective-permute-start(bf16[8,8,1024]{2,1,0:T(8,128)(2,1)} %get-tuple-element.18), channel_id=1, source_target_pairs={{0,7},{1,8},{2,9},{3,10},{4,11},{5,12},{6,13},{7,14},{8,15},{9,0},... | collective-permute-start | bytes 393224 | tf_op jit(solution)/shard_map/ppermute | solution.py:38
  71.1 5.9 %collective-permute-done.7 = bf16[8,8,1024]{2,1,0:T(8,128)(2,1)S(1)} collective-permute-done((bf16[8,8,1024]{2,1,0:T(8,128)(2,1)}, bf16[8,8,1024]{2,1,0:T(8,128)(2,1)S(1)}, u32[]{:S(2)}, u32[]{:S(2)}) %collective-permute-start.7) | collective-permute-done | bytes 131104 | tf_op jit(solution)/shard_map/ppermute | solution.py:38
  77.0 4.1 %collective-permute-done.8 = bf16[8,8,1024]{2,1,0:T(8,128)(2,1)S(1)} collective-permute-done((bf16[8,8,1024]{2,1,0:T(8,128)(2,1)}, bf16[8,8,1024]{2,1,0:T(8,128)(2,1)S(1)}, u32[]{:S(2)}, u32[]{:S(2)}) %collective-permute-start.8) | collective-permute-done | bytes 131104 | tf_op jit(solution)/shard_map/ppermute | solution.py:38
  81.1 1.6 collective-permute-start.10
  82.7 1.1 collective-permute-done.9
  83.8 1.7 collective-permute-start.11
  85.6 3.8 %collective-permute-done.10 = bf16[8,8,1024]{2,1,0:T(8,128)(2,1)S(1)} collective-permute-done((bf16[8,8,1024]{2,1,0:T(8,128)(2,1)S(1)}, bf16[8,8,1024]{2,1,0:T(8,128)(2,1)S(1)}, u32[]{:S(2)}, u32[]{:S(2)}) %collective-permute-start.10) | collective-permute-done | bytes 131104 | tf_op jit(solution)/shard_map/ppermute | solution.py:38
  89.4 2.9 %collective-permute-done.11 = bf16[8,8,1024]{2,1,0:T(8,128)(2,1)S(1)} collective-permute-done((bf16[8,8,1024]{2,1,0:T(8,128)(2,1)S(1)}, bf16[8,8,1024]{2,1,0:T(8,128)(2,1)S(1)}, u32[]{:S(2)}, u32[]{:S(2)}) %collective-permute-start.11) | collective-permute-done | bytes 131104 | tf_op jit(solution)/shard_map/ppermute | solution.py:38
  92.5 0.9 slice_dynamic-update-slice_fusion
  93.7 0.9 slice_dynamic-update-slice_fusion.1
  94.6 0.2 constant_dynamic-slice_fusion
  94.8 2.5 copy.24
  97.2 6.8 %gather_fusion.1 = bf16[32,128,1024]{2,1,0:T(8,128)(2,1)} fusion(bf16[128,8,1024]{2,0,1:T(8,128)(2,1)} %copy.24, s32[1024]{0:T(1024)} %pad_clamp_fusion), kind=kCustom, calls=%fused_computation.1 | custom fusion | bytes 16777344 | tf_op jit(solution)/shard_map/gather | solution.py:41
  104.1 4.8 %fusion.6 = (f32[8,128]{1,0:T(8,128)S(1)}, f32[8,128,4,128]{3,1,2,0:T(8,128)S(1)}) fusion(pred[8,4,128]{2,1,0:T(4,128)(4,1)S(1)} %broadcast_compare_fusion, bf16[128,8,4,1024]{3,0,2,1:T(8,128)(2,1)} %bitcast.81, bf16[8,128,1024,1]{2,1,3,0:T(8,128)(2,1)S(1)} %bitcast.76), kind=kOutput, calls=%fused_computation.14 | convolution fusion | flops 1074789376 | bytes 12591104 | tf_op jit(solution)/shard_map/grd,cgnd->grnc/dot_general | solution.py:43
  108.9 0.7 fusion.9
  109.6 2.5 fusion.24
  112.1 13.1 %fusion.2 = f32[128,8,1024]{2,1,0:T(8,128)} fusion(f32[128,32,1024]{2,0,1:T(8,128)S(1)} %bitcast.78, s32[32]{0:T(128)S(1)} %copy-done.10, s32[8]{0:T(128)S(1)} %copy-done.12), kind=kOutput, calls=%fused_computation.10 | convolution fusion | flops 402653440 | bytes 20971680 | tf_op jit(solution)/shard_map/cpd,pk->ckd/dot_general | solution.py:64
  125.2 10.6 %all-to-all-start = ((f32[128,8,1024]{2,1,0:T(8,128)}), f32[128,8,1024]{2,1,0:T(8,128)}, u32[]{:S(2)}, u32[]{:S(2)}) async-start(f32[128,8,1024]{2,1,0:T(8,128)} %fusion.2), calls=%async_computation | async-start | bytes 8388608 | tf_op jit(solution)/shard_map/all_to_all | solution.py:13
  135.8 0.2 compare_select_fusion.2
  136.1 14.8 %gather_fusion.2 = f32[1024]{0:T(1024)S(1)} fusion(f32[8,128,512]{1,2,0:T(8,128)} %bitcast.79, s32[1024]{0:T(1024)S(1)} %fusion.15), kind=kCustom, calls=%fused_computation.2 | custom fusion | bytes 20480 | tf_op jit(solution)/shard_map/jit(take_along_axis)/gather | solution.py:54
  151.0 0.7 bitcast_subtract_fusion.1
  151.7 7.3 %bitcast_convert_fusion = bf16[8,128,1024]{2,1,0:T(8,128)(2,1)} fusion(bf16[128,8,4,1024]{3,0,2,1:T(8,128)(2,1)} %bitcast.82, f32[8,128,4,128]{3,1,2,0:T(8,128)} %copy-done.2, s32[8,128]{1,0:T(8,128)S(1)} %add_select_fusion, s32[4,128]{1,0:T(4,128)S(1)} %multiply_add_fusion, f32[8,128]{1,0:T(8,128)S(1)} %fusion.9, f32[8,128]{1,0:T(8,128)S(1)} %get-tuple-element.29, ...), kind=kOutput, calls=%fused_computation.9 | convolution fusion | flops 1078460416 | bytes 12601344 | tf_op jit(solution)/shard_map/grnc,cgnd->grd/dot_general | solution.py:65
  159.0 69.2 %all-to-all-done = f32[128,8,1024]{2,1,0:T(8,128)} async-done(((f32[128,8,1024]{2,1,0:T(8,128)}), f32[128,8,1024]{2,1,0:T(8,128)}, u32[]{:S(2)}, u32[]{:S(2)}) %all-to-all-start) | async-done | bytes 4194336 | tf_op jit(solution)/shard_map/all_to_all | solution.py:13
  228.3 7.7 %copy.27 = f32[8,16,8,1024]{3,0,2,1:T(8,128)} copy(f32[8,16,8,1024]{3,2,0,1:T(8,128)} %bitcast.29) | data formatting | bytes 8388608 | tf_op jit(solution)/shard_map/all_to_all | solution.py:13
  236.0 2.5 broadcast_in_dim.50
  238.5 20.4 %scatter_fusion = f32[8,128,1024]{2,0,1:T(8,128)} fusion(f32[8,128,1024]{2,0,1:T(8,128)} %broadcast_in_dim.50, s32[128]{0:T(128)S(1)} %copy-done.8, f32[128,8,1024]{2,1,0:T(8,128)} %bitcast.80), kind=kCustom, calls=%fused_computation.4 | custom fusion | flops 1048576 | bytes 12583424 | tf_op jit(solution)/shard_map/scatter-add | solution.py:69
  258.9 2.5 convert_element_type.30
  261.4 2.5 copy.28
  (76 shorter events, 0.6 us)
Async XLA Ops:
  0.6 103.5 %copy-start = (bf16[1024,1024]{1,0:T(8,128)(2,1)S(1)}, bf16[1024,1024]{1,0:T(8,128)(2,1)}, u32[]{:S(2)}) copy-start(bf16[1024,1024]{1,0:T(8,128)(2,1)} %param.5) | copy-start | bytes 6291460
  1.7 34.2 %copy-start.9 = (s32[32]{0:T(128)}, s32[32]{0:T(128)S(1)}, u32[]{:S(2)}) copy-start(s32[32]{0:T(128)S(1)} %reshape.340) | copy-start | bytes 388
  6.3 29.6 %copy-start.11 = (s32[8]{0:T(128)}, s32[8]{0:T(128)S(1)}, u32[]{:S(2)}) copy-start(s32[8]{0:T(128)S(1)} %scatter_custom_fusion) | copy-start | bytes 100
  15.4 0.6 copy-start.7
  23.5 11.8 %copy-start.13 = (s32[8]{0:T(128)S(1)}, s32[8]{0:T(128)}, u32[]{:S(2)}) copy-start(s32[8]{0:T(128)} %param.8) | copy-start | bytes 100
  23.5 14.9 %copy-start.4 = (s32[1024]{0:T(1024)S(1)}, s32[1024]{0:T(1024)}, u32[]{:S(2)}) copy-start(s32[1024]{0:T(1024)} %param.9) | copy-start | bytes 12292
  26.3 1.3 copy-start.3
  28.6 63.8 %collective-permute-start.14 = (bf16[8,8,1024]{2,1,0:T(8,128)(2,1)S(1)}, bf16[8,8,1024]{2,1,0:T(8,128)(2,1)S(1)}, u32[]{:S(2)}, u32[]{:S(2)}) collective-permute-start(bf16[8,8,1024]{2,1,0:T(8,128)(2,1)S(1)} %get-tuple-element.12), channel_id=1, source_target_pairs={{0,1},{1,2},{2,3},{3,4},{4,5},{5,6},{6,7},{7,8},{8,9},{9,10},{10,1... | collective-permute-start | bytes 393224 | tf_op jit(solution)/shard_map/ppermute | solution.py:38
  32.6 59.8 %collective-permute-start.13 = (bf16[8,8,1024]{2,1,0:T(8,128)(2,1)S(1)}, bf16[8,8,1024]{2,1,0:T(8,128)(2,1)S(1)}, u32[]{:S(2)}, u32[]{:S(2)}) collective-permute-start(bf16[8,8,1024]{2,1,0:T(8,128)(2,1)S(1)} %get-tuple-element.13), channel_id=1, source_target_pairs={{0,2},{1,3},{2,4},{3,5},{4,6},{5,7},{6,8},{7,9},{8,10},{9,11},{10,... | collective-permute-start | bytes 393224 | tf_op jit(solution)/shard_map/ppermute | solution.py:38
  33.1 59.2 %collective-permute-start.12 = (bf16[8,8,1024]{2,1,0:T(8,128)(2,1)S(1)}, bf16[8,8,1024]{2,1,0:T(8,128)(2,1)S(1)}, u32[]{:S(2)}, u32[]{:S(2)}) collective-permute-start(bf16[8,8,1024]{2,1,0:T(8,128)(2,1)S(1)} %get-tuple-element.14), channel_id=1, source_target_pairs={{0,3},{1,4},{2,5},{3,6},{4,7},{5,8},{6,9},{7,10},{8,11},{9,12},{10... | collective-permute-start | bytes 393224 | tf_op jit(solution)/shard_map/ppermute | solution.py:38
  33.1 9.3 %collective-permute-start.1 = (bf16[8,8,1024]{2,1,0:T(8,128)(2,1)}, bf16[8,8,1024]{2,1,0:T(8,128)(2,1)S(1)}, u32[]{:S(2)}, u32[]{:S(2)}) collective-permute-start(bf16[8,8,1024]{2,1,0:T(8,128)(2,1)} %get-tuple-element.25), channel_id=1, source_target_pairs={{0,14},{1,15},{2,0},{3,1},{4,2},{5,3},{6,4},{7,5},{8,6},{9,7},{10,... | collective-permute-start | bytes 393224 | tf_op jit(solution)/shard_map/ppermute | solution.py:38
  34.0 8.4 %collective-permute-start = (bf16[8,8,1024]{2,1,0:T(8,128)(2,1)}, bf16[8,8,1024]{2,1,0:T(8,128)(2,1)S(1)}, u32[]{:S(2)}, u32[]{:S(2)}) collective-permute-start(bf16[8,8,1024]{2,1,0:T(8,128)(2,1)} %get-tuple-element.26), channel_id=1, source_target_pairs={{0,15},{1,0},{2,1},{3,2},{4,3},{5,4},{6,5},{7,6},{8,7},{9,8},{10,9... | collective-permute-start | bytes 393224 | tf_op jit(solution)/shard_map/ppermute | solution.py:38
  42.4 6.4 %collective-permute-start.2 = (bf16[8,8,1024]{2,1,0:T(8,128)(2,1)}, bf16[8,8,1024]{2,1,0:T(8,128)(2,1)S(1)}, u32[]{:S(2)}, u32[]{:S(2)}) collective-permute-start(bf16[8,8,1024]{2,1,0:T(8,128)(2,1)} %get-tuple-element.24), channel_id=1, source_target_pairs={{0,13},{1,14},{2,15},{3,0},{4,1},{5,2},{6,3},{7,4},{8,5},{9,6},{10... | collective-permute-start | bytes 393224 | tf_op jit(solution)/shard_map/ppermute | solution.py:38
  42.5 9.8 %collective-permute-start.3 = (bf16[8,8,1024]{2,1,0:T(8,128)(2,1)}, bf16[8,8,1024]{2,1,0:T(8,128)(2,1)S(1)}, u32[]{:S(2)}, u32[]{:S(2)}) collective-permute-start(bf16[8,8,1024]{2,1,0:T(8,128)(2,1)} %get-tuple-element.23), channel_id=1, source_target_pairs={{0,12},{1,13},{2,14},{3,15},{4,0},{5,1},{6,2},{7,3},{8,4},{9,5},{1... | collective-permute-start | bytes 393224 | tf_op jit(solution)/shard_map/ppermute | solution.py:38
  48.8 6.9 %collective-permute-start.4 = (bf16[8,8,1024]{2,1,0:T(8,128)(2,1)}, bf16[8,8,1024]{2,1,0:T(8,128)(2,1)S(1)}, u32[]{:S(2)}, u32[]{:S(2)}) collective-permute-start(bf16[8,8,1024]{2,1,0:T(8,128)(2,1)} %get-tuple-element.22), channel_id=1, source_target_pairs={{0,11},{1,12},{2,13},{3,14},{4,15},{5,0},{6,1},{7,2},{8,3},{9,4},{... | collective-permute-start | bytes 393224 | tf_op jit(solution)/shard_map/ppermute | solution.py:38
  52.3 7.3 %collective-permute-start.5 = (bf16[8,8,1024]{2,1,0:T(8,128)(2,1)}, bf16[8,8,1024]{2,1,0:T(8,128)(2,1)S(1)}, u32[]{:S(2)}, u32[]{:S(2)}) collective-permute-start(bf16[8,8,1024]{2,1,0:T(8,128)(2,1)} %get-tuple-element.21), channel_id=1, source_target_pairs={{0,10},{1,11},{2,12},{3,13},{4,14},{5,15},{6,0},{7,1},{8,2},{9,3},... | collective-permute-start | bytes 393224 | tf_op jit(solution)/shard_map/ppermute | solution.py:38
  55.7 12.3 %collective-permute-start.6 = (bf16[8,8,1024]{2,1,0:T(8,128)(2,1)}, bf16[8,8,1024]{2,1,0:T(8,128)(2,1)S(1)}, u32[]{:S(2)}, u32[]{:S(2)}) collective-permute-start(bf16[8,8,1024]{2,1,0:T(8,128)(2,1)} %get-tuple-element.20), channel_id=1, source_target_pairs={{0,9},{1,10},{2,11},{3,12},{4,13},{5,14},{6,15},{7,0},{8,1},{9,2},... | collective-permute-start | bytes 393224 | tf_op jit(solution)/shard_map/ppermute | solution.py:38
  59.5 17.5 %collective-permute-start.7 = (bf16[8,8,1024]{2,1,0:T(8,128)(2,1)}, bf16[8,8,1024]{2,1,0:T(8,128)(2,1)S(1)}, u32[]{:S(2)}, u32[]{:S(2)}) collective-permute-start(bf16[8,8,1024]{2,1,0:T(8,128)(2,1)} %get-tuple-element.19), channel_id=1, source_target_pairs={{0,8},{1,9},{2,10},{3,11},{4,12},{5,13},{6,14},{7,15},{8,0},{9,1},... | collective-permute-start | bytes 393224 | tf_op jit(solution)/shard_map/ppermute | solution.py:38
  68.0 13.1 %collective-permute-start.8 = (bf16[8,8,1024]{2,1,0:T(8,128)(2,1)}, bf16[8,8,1024]{2,1,0:T(8,128)(2,1)S(1)}, u32[]{:S(2)}, u32[]{:S(2)}) collective-permute-start(bf16[8,8,1024]{2,1,0:T(8,128)(2,1)} %get-tuple-element.18), channel_id=1, source_target_pairs={{0,7},{1,8},{2,9},{3,10},{4,11},{5,12},{6,13},{7,14},{8,15},{9,0},... | collective-permute-start | bytes 393224 | tf_op jit(solution)/shard_map/ppermute | solution.py:38
  77.0 6.8 %collective-permute-start.9 = (bf16[8,8,1024]{2,1,0:T(8,128)(2,1)S(1)}, bf16[8,8,1024]{2,1,0:T(8,128)(2,1)S(1)}, u32[]{:S(2)}, u32[]{:S(2)}) collective-permute-start(bf16[8,8,1024]{2,1,0:T(8,128)(2,1)S(1)} %get-tuple-element.17), channel_id=1, source_target_pairs={{0,6},{1,7},{2,8},{3,9},{4,10},{5,11},{6,12},{7,13},{8,14},{9,15},... | collective-permute-start | bytes 393224 | tf_op jit(solution)/shard_map/ppermute | solution.py:38
  81.1 8.3 %collective-permute-start.10 = (bf16[8,8,1024]{2,1,0:T(8,128)(2,1)S(1)}, bf16[8,8,1024]{2,1,0:T(8,128)(2,1)S(1)}, u32[]{:S(2)}, u32[]{:S(2)}) collective-permute-start(bf16[8,8,1024]{2,1,0:T(8,128)(2,1)S(1)} %get-tuple-element.16), channel_id=1, source_target_pairs={{0,5},{1,6},{2,7},{3,8},{4,9},{5,10},{6,11},{7,12},{8,13},{9,14},{... | collective-permute-start | bytes 393224 | tf_op jit(solution)/shard_map/ppermute | solution.py:38
  83.8 8.5 %collective-permute-start.11 = (bf16[8,8,1024]{2,1,0:T(8,128)(2,1)S(1)}, bf16[8,8,1024]{2,1,0:T(8,128)(2,1)S(1)}, u32[]{:S(2)}, u32[]{:S(2)}) collective-permute-start(bf16[8,8,1024]{2,1,0:T(8,128)(2,1)S(1)} %get-tuple-element.15), channel_id=1, source_target_pairs={{0,4},{1,5},{2,6},{3,7},{4,8},{5,9},{6,10},{7,11},{8,12},{9,13},{1... | collective-permute-start | bytes 393224 | tf_op jit(solution)/shard_map/ppermute | solution.py:38
  108.9 3.2 %copy-start.2 = (f32[8,128,4,128]{3,1,2,0:T(8,128)}, f32[8,128,4,128]{3,1,2,0:T(8,128)S(1)}, u32[]{:S(2)}) copy-start(f32[8,128,4,128]{3,1,2,0:T(8,128)S(1)} %get-tuple-element.30) | copy-start | bytes 6291460
  109.6 2.5 copy-start.10
  109.6 2.5 copy-start.12
  125.2 10.6 %copy-start.5 = (s32[8]{0:T(128)S(1)}, s32[8]{0:T(128)}, u32[]{:S(2)}) copy-start(s32[8]{0:T(128)} %get-tuple-element.28) | copy-start | bytes 100
  125.2 10.6 %copy-start.6 = (pred[8]{0:T(512)(128)(4,1)S(1)}, pred[8]{0:T(512)(128)(4,1)}, u32[]{:S(2)}) copy-start(pred[8]{0:T(512)(128)(4,1)} %broadcast_compare_fusion.1) | copy-start | bytes 28
  125.2 103.0 %all-to-all-start = ((f32[128,8,1024]{2,1,0:T(8,128)}), f32[128,8,1024]{2,1,0:T(8,128)}, u32[]{:S(2)}, u32[]{:S(2)}) async-start(f32[128,8,1024]{2,1,0:T(8,128)} %fusion.2), calls=%async_computation | async-start | bytes 8388608 | tf_op jit(solution)/shard_map/all_to_all | solution.py:13
  236.0 2.5 copy-start.8
  238.5 25.4 %copy-start.1 = (bf16[1024,1024]{1,0:T(8,128)(2,1)S(1)}, bf16[1024,1024]{1,0:T(8,128)(2,1)}, u32[]{:S(2)}) copy-start(bf16[1024,1024]{1,0:T(8,128)(2,1)} %param.5) | copy-start | bytes 6291460
